TPU v7x, 32 devices: a whole 2x2x4 slice. The times are simulated.
32 devices in a mesh: space: 16 (over z, y, core), dp: 2 (over x).
Axes of the slice: x: 2, y: 2, z: 4, core: 2. Of those that a mesh axis runs over, the one named last changes fastest.
Arguments:
- node_features: float32 [2, 128, 4096], P('dp', None, 'space'), may hold values from -6 to 6
- positions: float32 [2, 3, 4096], P('dp', None, 'space')
- species: int32 [2, 4096], P('dp', 'space'), may hold values from 0 to 7
- energy_cotangent: float32 [2, 4096], P('dp', 'space'), may hold values from -6 to 6
- pair_target: int32 [2, 320], P('dp', 'space'), may hold values from 0 to 3, as said below
- pair_source: int32 [2, 320], P('dp', 'space'), may hold values from 0 to 7, as said below
- pair_count: int32 [2, 16], P('dp', 'space'), may hold values from 4 to 20, as said below
- radial_weight: float32 [8, 128], replicated, may hold values from -2 to 2
- mix_weight: bfloat16 [384, 128], replicated, may hold values from -0.3125 to 0.3125
- readout_weight: float32 [128], replicated, may hold values from -0.5 to 0.5
- species_shift: float32 [8], replicated, may hold values from -4 to 4
Outputs:
- atom_energy: float32 [2, 4096], P('dp', 'space')
- feature_grad: float32 [2, 128, 4096], P('dp', None, 'space')
- radial_grad: float32 [8, 128], replicated
- mix_grad: float32 [384, 128], replicated
- readout_grad: float32 [128], replicated
- shift_grad: float32 [8], replicated
Inputs may be any that keep to these rules, and one draw needn't show every extreme that they name: `pair_target`: the target cell of a slot lies in its slab. `pair_source`: A live slot's source cell lies within 2 cells of its target cell and inside the snapshot; every target cell pairs with itself; no pair appears twice in a slab. `pair_count`: counts differ from slab to slab; in every snapshot some slab uses all 20 slots.
All inputs are finite; a program needn't handle non-finite values.
Results may differ from a plain program's by a relative error of at most 0.0009.
The roundings to bfloat16 on the way count: a program that leaves them out, or rounds other values in their place, can miss the bound.
Values sent between devices are 32-bit elements; how exact they have to be, the bound alone decides.
No kernel may reach another device: no remote copies, remote signals or barrier semaphores. Data moves between devices by JAX's collectives and lax.ppermute only.
A program may use at most 64 MiB of HBM per device.

v0:
```python
import functools
import math

import jax
import jax.numpy as jnp
from jax import lax
from jax.experimental import pallas as pl
from jax.experimental.pallas import tpu as pltpu
from jax.sharding import PartitionSpec as P

CH = 128
NB = 8
NY = 9
NSPEC = 8
CELL_ATOMS = 64
HALO_CELLS = 2
GROUP = 2 * CELL_ATOMS
ROWS = 16

cutoff = 5.0
message_scale = 0.25

COS_COEFFS = (
    0.9999999998846169,
    -4.934802185771876,
    4.058711815779763,
    -1.3352602773967561,
    0.23532080049888648,
    -0.025785772074137014,
    0.0019043022864480008,
    -8.868331860867329e-05,
)
SINC_COEFFS = (
    0.9999999992502204,
    -1.6449339933418936,
    0.8117412468909989,
    -0.1907447263221115,
    0.02612742969685046,
    -0.0023157632409761065,
    0.00012580778956459784,
)

MIX_ROWS = 3 * CH
HALF = MIX_ROWS // 2
QUARTER = MIX_ROWS // 4
REST = 16
CELLS = 4 + 2 * HALO_CELLS
LOCAL = ((0, 1), (0, 2), (1, 0), (1, 1))
SMALL = 8
SLAB_ROWS = CH + 8


def polynomial(coeffs, x):
    total = coeffs[-1] * x + coeffs[-2]
    for c in coeffs[-3::-1]:
        total = total * x + c
    return total


def factor_rows(factor_ref, row, source, target, keep):
    dx = (target[0] - source[0]) * (1.0 / cutoff)
    dy = (target[1] - source[1]) * (1.0 / cutoff)
    dz = (target[2] - source[2]) * (1.0 / cutoff)
    xx, yy, zz = dx * dx, dy * dy, dz * dz
    square = xx + yy + zz
    inside = jnp.minimum(square, 1.0)
    gap = 1.0 - inside
    base = (gap * gap) * keep * polynomial(SINC_COEFFS, inside)
    twice_cos = polynomial([2.0 * c for c in COS_COEFFS], inside)
    raw = [base, twice_cos * base]
    for _ in range(NB - 2):
        raw.append(twice_cos * raw[-1] - raw[-2])
    radial = [value if b == 0 else value * (1.0 / (b + 1)) for b, value in enumerate(raw)]
    root_three = math.sqrt(3.0)
    root_fifteen = math.sqrt(15.0)
    root_five = math.sqrt(5.0)
    wide_x = root_fifteen * dx
    harmonic = [
        None,
        root_three * dx,
        root_three * dy,
        root_three * dz,
        wide_x * dy,
        (root_fifteen * dy) * dz,
        (0.5 * root_five) * (3.0 * zz - square),
        wide_x * dz,
        (0.5 * root_fifteen) * (xx - yy),
    ]
    for b in range(NB):
        rows = slice(b * GROUP + row, b * GROUP + row + ROWS)
        for y in range(NY):
            value = radial[b] if y == 0 else radial[b] * harmonic[y]
            factor_ref[rows, y * GROUP : (y + 1) * GROUP] = value.astype(jnp.bfloat16)


def column_to_row(column, size):
    wide = jnp.broadcast_to(column, (size, GROUP))
    at = lax.broadcasted_iota(jnp.int32, (size, GROUP), 0)
    lane = lax.broadcasted_iota(jnp.int32, (size, GROUP), 1)
    return jnp.sum(jnp.where(at == lane, wide, 0.0), axis=0, keepdims=True)


def split_kernel(*refs):
    features_ref, place_in_ref, *inputs = refs[:SMALL + 2]
    pair_ref, cross_ref, *outputs = refs[SMALL + 2 : 2 * SMALL + 4]
    place_ref, sems = refs[2 * SMALL + 4 :]
    core = lax.axis_index("space") % 2
    place_copy = pltpu.make_async_copy(place_in_ref, place_ref, sems.at[2])
    place_copy.start()
    copies = []
    for k, (ref, side) in enumerate(((pair_ref, 1 - core), (cross_ref, core))):
        at = pl.ds(pl.multiple_of(side * GROUP, GROUP), GROUP)
        copies.append(
            pltpu.make_async_copy(features_ref.at[0, :, at], ref.at[pl.ds(0, CH)], sems.at[k])
        )
    for k, (src, dst) in enumerate(zip(inputs, outputs)):
        copies.append(pltpu.make_async_copy(src, dst, sems.at[3 + k]))
    for copy in copies:
        copy.start()
    place_copy.wait()
    low, high = slice(GROUP), slice(GROUP, 2 * GROUP)
    filler = jnp.zeros((5, GROUP), jnp.float32)
    for ref, one, two in ((pair_ref, high, low), (cross_ref, low, high)):
        rows = [
            jnp.where(core == 0, place_ref[axis, :, one], place_ref[axis, :, two]) for axis in range(3)
        ]
        ref[CH:, :] = jnp.concatenate(rows + [filler], axis=0)
    for copy in copies:
        copy.wait()


def live_flags(count, pair_target, pair_source):
    size = (4 * CELLS, pair_target.shape[1])
    at = lax.broadcasted_iota(jnp.int32, size, 0)
    slot = lax.broadcasted_iota(jnp.int32, size, 1)
    hit = (pair_target * CELLS + pair_source == at) & (slot < count)
    return jnp.max(jnp.where(hit, message_scale, 0.0), axis=1, keepdims=True)


def keep_rows(flags, t, d):
    lane = lax.broadcasted_iota(jnp.int32, (1, GROUP), 1)
    rows = []
    for scell in (2 * (t + d), 2 * (t + d) + 1):
        one, two = [(2 * t + k) * CELLS + scell for k in range(2)]
        rows.append(jnp.where(lane < CELL_ATOMS, flags[one : one + 1], flags[two : two + 1]))
    return rows


def set_source(scaled_ref, place_ref, slab, weight_t):
    features = slab[:CH]
    for b in range(NB):
        scaled_ref[:, b * GROUP : (b + 1) * GROUP] = (features * weight_t[:, b : b + 1]).astype(
            jnp.bfloat16
        )
    place = slab[CH:].T
    for axis in range(3):
        place_ref[axis] = jnp.broadcast_to(place[:, axis : axis + 1], (GROUP, GROUP))


def fill_block(factor_ref, place_ref, keeps, target, d):
    row_at = lax.broadcasted_iota(jnp.int32, (ROWS, GROUP), 0)
    lane_at = lax.broadcasted_iota(jnp.int32, (ROWS, GROUP), 1)
    for half in range(2):
        for row in range(half * CELL_ATOMS, (half + 1) * CELL_ATOMS, ROWS):
            source = [place_ref[axis, row : row + ROWS, :] for axis in range(3)]
            keep = jnp.broadcast_to(keeps[half], (ROWS, GROUP))
            if d == 1:
                keep = jnp.where(row_at + row == lane_at, 0.0, keep)
            factor_rows(factor_ref, row, source, target, keep)


def local_kernel(
    count_ref,
    pair_target_ref,
    pair_source_ref,
    radial_ref,
    pair_ref,
    cross_ref,
    factor_ref,
    messages_ref,
    keep_ref,
    scaled_ref,
    place_ref,
):
    even = lax.axis_index("space") % 2 == 0
    slabs = (
        jnp.where(even, cross_ref[...], pair_ref[...]),
        jnp.where(even, pair_ref[...], cross_ref[...]),
    )
    targets = [[slab[CH + axis : CH + axis + 1] for axis in range(3)] for slab in slabs]
    flags = live_flags(count_ref[0, 0], pair_target_ref[...], pair_source_ref[...])
    weight_t = radial_ref[...].T
    for g in range(2):
        set_source(scaled_ref.at[g], place_ref.at[g], slabs[g], weight_t)

    def fill(block):
        t, d = LOCAL[block]
        fill_block(factor_ref.at[block], place_ref.at[t + d - 1], keep_rows(flags, t, d), targets[t], d)

    totals = [None, None]
    fill(0)
    for block, (t, d) in enumerate(LOCAL):
        product = jnp.dot(
            scaled_ref[t + d - 1], factor_ref[block], preferred_element_type=jnp.float32
        )
        totals[t] = product if totals[t] is None else totals[t] + product
        if block + 1 < len(LOCAL):
            fill(block + 1)
    for t in range(2):
        messages_ref[t] = totals[t]
    keep_ref[...] = jnp.concatenate(
        keep_rows(flags, 0, 0) + keep_rows(flags, 1, 2) + [jnp.zeros((4, GROUP), jnp.float32)], axis=0
    )


def node_kernel(
    scale,
    pair_ref,
    cross_ref,
    from_pair_ref,
    from_cross_ref,
    messages_ref,
    keep_ref,
    species_ref,
    shift_ref,
    energy_grad_ref,
    radial_ref,
    mix_ref,
    readout_ref,
    energy_ref,
    spread_ref,
    kept_ref,
    sent_ref,
    rest_ref,
    grad_messages_ref,
    halo_ref,
    scaled_ref,
    place_ref,
):
    even = lax.axis_index("space") % 2 == 0
    weight_t = radial_ref[...].T
    slabs = (
        jnp.where(even, from_cross_ref[...], from_pair_ref[...]),
        jnp.where(even, cross_ref[...], pair_ref[...]),
        jnp.where(even, pair_ref[...], cross_ref[...]),
        jnp.where(even, from_pair_ref[...], from_cross_ref[...]),
    )
    targets = [[slab[CH + axis : CH + axis + 1] for axis in range(3)] for slab in slabs[1:3]]

    def fill(t):
        d = 2 * t
        set_source(scaled_ref.at[t], place_ref.at[t], slabs[t + d], weight_t)
        keeps = [keep_ref[2 * t + half : 2 * t + half + 1, :] for half in range(2)]
        fill_block(halo_ref.at[t], place_ref.at[t], keeps, targets[t], d)

    def add_halo(t):
        return messages_ref[t] + jnp.dot(
            scaled_ref[t], halo_ref[t], preferred_element_type=jnp.float32
        )

    readout = jnp.broadcast_to(readout_ref[...], (8, CH)).T[:, :1]
    mix = mix_ref[...]
    mix_t = mix.astype(jnp.float32).T.astype(jnp.bfloat16)

    def node_stage(t, messages):
        at = slice(t * GROUP, (t + 1) * GROUP)
        part = [messages[:, y * GROUP : (y + 1) * GROUP] for y in range(NY)]
        invariants = jnp.concatenate(
            [
                part[0],
                0.5 * (part[1] * part[1] + part[2] * part[2] + part[3] * part[3]),
                0.5
                * (
                    part[4] * part[4]
                    + part[5] * part[5]
                    + part[6] * part[6]
                    + part[7] * part[7]
                    + part[8] * part[8]
                ),
            ],
            axis=0,
        ).astype(jnp.bfloat16)
        preact = jnp.dot(mix_t, invariants, preferred_element_type=jnp.float32)
        gating = jax.nn.sigmoid(preact)
        updated = slabs[t + 1][:CH] + preact * gating
        energy_grad = energy_grad_ref[:, at]
        kinds = species_ref[:, at]
        shifts = jnp.zeros((1, GROUP), jnp.float32)
        for n in range(NSPEC):
            shifts = jnp.where(kinds == n, shift_ref[:, n : n + 1], shifts)
        energy_ref[:, at] = jnp.sum(updated * readout, axis=0, keepdims=True) + shifts
        spread = readout * energy_grad
        spread_ref[:, at] = spread
        grad_pre = (spread * gating * (1.0 + preact * (1.0 - gating))).astype(jnp.bfloat16)
        grad_mix = lax.dot_general(
            invariants, grad_pre, (((1,), (1,)), ((), ())), preferred_element_type=jnp.float32
        )
        grad_inv = jnp.dot(mix, grad_pre, preferred_element_type=jnp.float32)
        grad_messages_ref[t] = jnp.concatenate(
            [grad_inv[:CH]]
            + [grad_inv[CH : 2 * CH] * part[y] for y in range(1, 4)]
            + [grad_inv[2 * CH :] * part[y] for y in range(4, NY)],
            axis=1,
        ).astype(jnp.bfloat16)
        return updated * energy_grad, grad_mix

    fill(0)
    first = add_halo(0)
    fill(1)
    out_low, mix_low = node_stage(0, first)
    out_high, mix_high = node_stage(1, add_halo(1))

    grad_mix = (mix_low + mix_high) * scale
    kept_ref[...] = jnp.where(even, grad_mix[:HALF], grad_mix[HALF:])
    sent_ref[...] = jnp.where(even, grad_mix[HALF:], grad_mix[:HALF])
    readout_row = column_to_row(jnp.sum(out_low + out_high, axis=1, keepdims=True), CH)
    here = lax.broadcasted_iota(jnp.int32, (NSPEC, 2 * GROUP), 0) == species_ref[...]
    by_kind = jnp.sum(jnp.where(here, energy_grad_ref[...], 0.0), axis=1, keepdims=True)
    rest_ref[...] = jnp.concatenate(
        [readout_row, column_to_row(by_kind, NSPEC), jnp.zeros((6, CH), jnp.float32)], axis=0
    )


def back(factor, grad_messages):
    return lax.dot_general(
        factor, grad_messages, (((1,), (1,)), ((), ())), preferred_element_type=jnp.float32
    )


def source_grads(total, features, weight):
    features_t = features.T
    grad_t = None
    radial = []
    for b in range(NB):
        piece = total[b * GROUP : (b + 1) * GROUP]
        term = piece * weight[b : b + 1, :]
        grad_t = term if grad_t is None else grad_t + term
        radial.append(jnp.sum(piece * features_t, axis=0, keepdims=True))
    return grad_t.T, jnp.concatenate(radial, axis=0)


def halo_back_kernel(
    halo_ref, grad_messages_ref, from_pair_ref, from_cross_ref, radial_ref, to_pair_ref, to_cross_ref, share_ref
):
    even = lax.axis_index("space") % 2 == 0
    weight = radial_ref[...]
    before = jnp.where(even, from_cross_ref[:CH, :], from_pair_ref[:CH, :])
    after = jnp.where(even, from_pair_ref[:CH, :], from_cross_ref[:CH, :])
    grad_before, share_before = source_grads(back(halo_ref[0], grad_messages_ref[0]), before, weight)
    grad_after, share_after = source_grads(back(halo_ref[1], grad_messages_ref[1]), after, weight)
    to_pair_ref[...] = jnp.where(even, grad_after, grad_before)
    to_cross_ref[...] = jnp.where(even, grad_before, grad_after)
    share_ref[...] = share_before + share_after


def own_back_kernel(
    scale,
    local_ref,
    grad_messages_ref,
    pair_ref,
    cross_ref,
    radial_ref,
    share_ref,
    rest_ref,
    spread_ref,
    own_grad_ref,
    joined_ref,
):
    even = lax.axis_index("space") % 2 == 0
    weight = radial_ref[...]
    low = jnp.where(even, cross_ref[:CH, :], pair_ref[:CH, :])
    high = jnp.where(even, pair_ref[:CH, :], cross_ref[:CH, :])
    share = share_ref[...]
    for g, features in enumerate((low, high)):
        total = back(local_ref[g], grad_messages_ref[0]) + back(local_ref[2 + g], grad_messages_ref[1])
        grad, part = source_grads(total, features, weight)
        at = slice(g * GROUP, (g + 1) * GROUP)
        own_grad_ref[:, at] = spread_ref[:, at] + grad
        share = share + part
    joined_ref[:NB, :] = share * scale
    joined_ref[NB:, :] = rest_ref[...] * scale


def quarter_kernel(kept_ref, received_ref, keep_ref, send_ref):
    first = lax.axis_index("dp") % 2 == 0
    low = kept_ref[:QUARTER, :] + received_ref[:QUARTER, :]
    high = kept_ref[QUARTER:, :] + received_ref[QUARTER:, :]
    keep_ref[...] = jnp.where(first, low, high)
    send_ref[...] = jnp.where(first, high, low)


def join_kernel(kept_ref, received_ref, rest_ref, out_ref):
    out_ref[:QUARTER, :] = kept_ref[...] + received_ref[...]
    out_ref[QUARTER:, :] = rest_ref[...]


def gather_kernel(mine_ref, other_ref, out_ref):
    first = lax.axis_index("dp") % 2 == 0
    mine, other = mine_ref[:QUARTER, :], other_ref[:QUARTER, :]
    out_ref[:QUARTER, :] = jnp.where(first, mine, other)
    out_ref[QUARTER:HALF, :] = jnp.where(first, other, mine)
    out_ref[HALF:, :] = mine_ref[QUARTER:, :] + other_ref[QUARTER:, :]


def fold_kernel(own_ref, from_pair_ref, from_cross_ref, energy_in_ref, grad_ref, energy_ref):
    even = lax.axis_index("space") % 2 == 0
    pair = from_pair_ref[...]
    cross = from_cross_ref[...]
    grad_ref[0, :, :GROUP] = own_ref[:, :GROUP] + jnp.where(even, cross, pair)
    grad_ref[0, :, GROUP:] = own_ref[:, GROUP:] + jnp.where(even, pair, cross)
    energy_ref[...] = energy_in_ref[...]


def finish_kernel(mine_ref, other_ref, radial_ref, mix_ref, readout_ref, shift_ref):
    even = lax.axis_index("space") % 2 == 0
    mine, other = mine_ref[:HALF, :], other_ref[:HALF, :]
    mix_ref[:HALF, :] = jnp.where(even, mine, other)
    mix_ref[HALF:, :] = jnp.where(even, other, mine)
    rest = mine_ref[HALF:, :] + other_ref[HALF:, :]
    radial_ref[...] = rest[:NB]
    readout_ref[...] = rest[NB : NB + 1]
    shift_ref[...] = rest[NB + 1 : NB + 2, :NSPEC]


def exchange_routes(space, dp):
    steps = [(1 << k, 0) for k in range(1, space.bit_length() - 1)]
    steps += [(0, 1 << k) for k in range(1, dp.bit_length() - 1)]
    routes = []
    for turn in range(len(steps)):
        route = []
        for s in range(space):
            across, along = steps[(turn + s % 2) % len(steps)]
            for d in range(dp):
                route.append((s * dp + d, (s ^ across) * dp + (d ^ along)))
        routes.append(route)
    return routes


def call(kernel, name, inputs, outputs, mib=4, scratch=(), flops=0):
    vmem = pl.BlockSpec(memory_space=pltpu.VMEM)
    shapes = tuple(jax.ShapeDtypeStruct(shape, kind) for shape, kind in outputs)
    moved = sum(math.prod(v.shape) * v.dtype.itemsize for v in (*inputs, *shapes))
    return pl.pallas_call(
        kernel,
        out_shape=shapes,
        in_specs=[vmem] * len(inputs),
        out_specs=(vmem,) * len(shapes),
        scratch_shapes=scratch,
        compiler_params=pltpu.CompilerParams(vmem_limit_bytes=mib * 1024 * 1024),
        cost_estimate=pl.CostEstimate(flops=flops, bytes_accessed=moved, transcendentals=0),
        name=name,
    )(*inputs)


def in_hbm(value):
    return pltpu.with_memory_space_constraint(value, pltpu.HBM)


def body(
    node_features,
    positions,
    species,
    energy_cotangent,
    pair_target,
    pair_source,
    pair_count,
    radial_weight,
    mix_weight,
    readout_weight,
    species_shift,
):
    atoms_here = node_features.shape[2]
    space, dp = lax.axis_size("space"), lax.axis_size("dp")
    scale = 1.0 / math.sqrt(atoms_here * space * dp)
    pair = [(i, i ^ 1) for i in range(space)]
    cross = [(i, ((i + 1) ^ 1) - 1) for i in range(1, space - 1)]

    across = [(i, i ^ 1) for i in range(dp)]
    hbm = pl.BlockSpec(memory_space=pltpu.HBM)
    smem = pl.BlockSpec(memory_space=pltpu.SMEM)
    vmem = pl.BlockSpec(memory_space=pltpu.VMEM)
    f32, bf16 = jnp.float32, jnp.bfloat16
    slab = jax.ShapeDtypeStruct((SLAB_ROWS, GROUP), f32)
    small = (
        pair_target,
        pair_source,
        species,
        species_shift.reshape(1, NSPEC),
        energy_cotangent,
        radial_weight,
        mix_weight,
        readout_weight.reshape(1, CH),
    )
    to_pair, to_cross, *small = pl.pallas_call(
        split_kernel,
        out_shape=(slab, slab) + tuple(jax.ShapeDtypeStruct(v.shape, v.dtype) for v in small),
        in_specs=[hbm] * (SMALL + 2),
        out_specs=(vmem,) * (SMALL + 2),
        scratch_shapes=[
            pltpu.VMEM((3, 1, atoms_here), f32),
            pltpu.SemaphoreType.DMA((SMALL + 3,)),
        ],
        compiler_params=pltpu.CompilerParams(vmem_limit_bytes=4 * 1024 * 1024),
        name="split",
    )(
        in_hbm(node_features),
        in_hbm(jnp.transpose(positions, (1, 0, 2))),
        *[in_hbm(v) for v in small],
    )
    targets, sources, species, shift, energy_grad, radial, mix, readout = small
    from_cross = lax.ppermute(to_cross, "space", cross)
    from_pair = lax.ppermute(to_pair, "space", pair)

    block_flops = 2 * CH * NB * NY * GROUP * GROUP
    local_factor, messages, keep = pl.pallas_call(
        local_kernel,
        out_shape=(
            jax.ShapeDtypeStruct((len(LOCAL), NB * GROUP, NY * GROUP), bf16),
            jax.ShapeDtypeStruct((2, CH, NY * GROUP), f32),
            jax.ShapeDtypeStruct((8, GROUP), f32),
        ),
        in_specs=[smem] + [vmem] * 5,
        out_specs=(vmem,) * 3,
        scratch_shapes=[
            pltpu.VMEM((2, CH, NB * GROUP), bf16),
            pltpu.VMEM((2, 3, GROUP, GROUP), f32),
        ],
        compiler_params=pltpu.CompilerParams(vmem_limit_bytes=16 * 1024 * 1024),
        cost_estimate=pl.CostEstimate(
            flops=len(LOCAL) * block_flops, bytes_accessed=14_000_000, transcendentals=0
        ),
        name="local_pairs",
    )(pair_count, targets, sources, radial, to_pair, to_cross)

    energy, spread, kept, sent, rest, grad_messages, halo_factor = call(
        functools.partial(node_kernel, scale),
        "node_stage",
        (
            to_pair,
            to_cross,
            from_pair,
            from_cross,
            messages,
            keep,
            species,
            shift,
            energy_grad,
            radial,
            mix,
            readout,
        ),
        (
            ((1, atoms_here), f32),
            ((CH, atoms_here), f32),
            ((HALF, CH), f32),
            ((HALF, CH), f32),
            ((8, CH), f32),
            ((2, CH, NY * GROUP), bf16),
            ((2, NB * GROUP, NY * GROUP), bf16),
        ),
        16,
        [pltpu.VMEM((2, CH, NB * GROUP), bf16), pltpu.VMEM((2, 3, GROUP, GROUP), f32)],
        2 * block_flops,
    )

    received = lax.ppermute(sent, "space", pair)
    pair_grad, cross_grad, share = call(
        halo_back_kernel,
        "halo_back",
        (halo_factor, grad_messages, from_pair, from_cross, radial),
        (((CH, GROUP), f32), ((CH, GROUP), f32), ((NB, CH), f32)),
        12,
        (),
        2 * block_flops,
    )
    received, share = lax.optimization_barrier((received, share))
    quarter, sent = call(
        quarter_kernel,
        "quarter",
        (kept, received),
        (((QUARTER, CH), f32), ((QUARTER, CH), f32)),
    )
    sent, grad_messages = lax.optimization_barrier((sent, grad_messages))
    received = lax.ppermute(sent, "dp", across)
    own_grad, joined = call(
        functools.partial(own_back_kernel, scale),
        "own_back",
        (local_factor, grad_messages, to_pair, to_cross, radial, share, rest, spread),
        (((CH, atoms_here), f32), ((REST, CH), f32)),
        12,
        (),
        4 * block_flops,
    )
    (value,) = call(
        join_kernel, "join", (quarter, received, joined), (((QUARTER + REST, CH), f32),)
    )
    for turn, route in enumerate(exchange_routes(space, dp)):
        if turn == 0:
            value, cross_grad = lax.optimization_barrier((value, cross_grad))
            cross_grad = lax.ppermute(cross_grad, "space", cross)
        if turn == 1:
            value, cross_grad, pair_grad = lax.optimization_barrier((value, cross_grad, pair_grad))
            pair_grad = lax.ppermute(pair_grad, "space", pair)
        if turn == 2:
            value, pair_grad = lax.optimization_barrier((value, pair_grad))
        value = value + lax.ppermute(value, ("space", "dp"), route)
    (value,) = call(
        gather_kernel,
        "gather",
        (value, lax.ppermute(value, "dp", across)),
        (((HALF + REST, CH), f32),),
    )
    feature_grad, energy = call(
        fold_kernel,
        "fold",
        (own_grad, pair_grad, cross_grad, energy),
        (((1, CH, atoms_here), f32), ((1, atoms_here), f32)),
    )
    radial_grad, mix_grad, readout_grad, shift_grad = call(
        finish_kernel,
        "finish",
        (value, lax.ppermute(value, "space", pair)),
        (((NB, CH), f32), ((MIX_ROWS, CH), f32), ((1, CH), f32), ((1, NSPEC), f32)),
    )
    return (
        energy,
        feature_grad,
        radial_grad,
        mix_grad,
        readout_grad.reshape(CH),
        shift_grad.reshape(NSPEC),
    )


def solution(mesh):
    return jax.shard_map(
        body,
        mesh=mesh,
        in_specs=(
            P("dp", None, "space"),
            P("dp", None, "space"),
            P("dp", "space"),
            P("dp", "space"),
            P("dp", "space"),
            P("dp", "space"),
            P("dp", "space"),
            P(),
            P(),
            P(),
            P(),
        ),
        out_specs=(P("dp", "space"), P("dp", None, "space"), P(), P(), P(), P()),
        check_vma=False,
    )
```

profile of v0, /device:TPU:0, one launch (start us, length us, event | category | flops | bytes accessed | tf_op | source)
XLA Modules:
  0.0 43.5 jit_solution(3047740431195325229)
XLA Ops:
  0.6 1.2 %split.1 = (f32[136,128]{1,0:T(8,128)S(1)}, f32[136,128]{1,0:T(8,128)S(1)}, s32[1,20]{1,0:T(1,128)S(1)}, s32[1,20]{1,0:T(1,128)S(1)}, s32[1,256]{1,0:T(1,128)S(1...) custom-call(f32[1,128,256]{2,1,0:T(8,128)} %refs_0_.1, ...), custom_call_target="tpu_custom_call" | custom-call | tf_op jit(solution)/shard_map/split/pallas_call | solution.py:494
  1.8 0.5 %collective-permute-start = (f32[136,128]{1,0:T(8,128)S(1)}, f32[136,128]{1,0:T(8,128)S(1)}, u32[]{:S(2)}, u32[]{:S(2)}) collective-permute-start(f32[136,128]{1,0:T(8,128)S(1)} %get-tuple-element.53.pair_ref), channel_id=1, source_target_pairs={{0,2},{2,0},{4,6},{6,4},{8,10},{10,8},{12,14},{14,12},{16,18},{18,... | collective-permute-start | bytes 208904 | tf_op jit(solution)/shard_map/ppermute | solution.py:512
  2.3 0.7 %collective-permute-start.1 = (f32[136,128]{1,0:T(8,128)S(1)}, f32[136,128]{1,0:T(8,128)S(1)}, u32[]{:S(2)}, u32[]{:S(2)}) collective-permute-start(f32[136,128]{1,0:T(8,128)S(1)} %get-tuple-element.54.cross_ref), channel_id=1, source_target_pairs={{2,4},{4,2},{6,8},{8,6},{10,12},{12,10},{14,16},{16,14},{18,20},{2... | collective-permute-start | bytes 208904 | tf_op jit(solution)/shard_map/ppermute | solution.py:511
  3.7 4.4 %local_pairs.1 = (bf16[4,1024,1152]{2,1,0:T(8,128)(2,1)S(1)}, f32[2,128,1152]{2,1,0:T(8,128)S(1)}, f32[8,128]{1,0:T(8,128)S(1)}) custom-call(s32[1,1]{1,0:T(1,128)S(6)} %copy.17.count_ref, s32[1,20]{1,0:T(1,128)S(1)} %get-tuple-element.50.pair_target_ref, s32[1,20]{1,0:T(1,128)S(1)} %get-tuple-element.51.pair_source_ref, ...), custom_call_target="tpu_custom_call" | custom-call | flops 1207959552 | bytes 14000000 | tf_op jit(solution)/shard_map/local_pairs/pallas_call | solution.py:515
  8.1 0.0 collective-permute-done.from_pair_ref
  8.1 0.0 collective-permute-done.1.from_cross_ref
  8.1 2.9 %node_stage.1 = (f32[1,256]{1,0:T(1,128)S(1)}, f32[128,256]{1,0:T(8,128)S(1)}, f32[192,128]{1,0:T(8,128)S(1)}, f32[192,128]{1,0:T(8,128)S(1)}, f32[8,128]{1,0:T(...) custom-call(f32[136,128]{1,0:T(8,128)S(1)} %get-tuple-element.53.pair_ref, ...), custom_call_target="tpu_custom_call" | custom-call | flops 603979776 | bytes 7208480 | tf_op jit(solution)/shard_map/node_stage/pallas_call | solution.py:443
  11.0 4.0 %collective-permute-start.2 = (f32[192,128]{1,0:T(8,128)S(1)}, f32[192,128]{1,0:T(8,128)S(1)}, u32[]{:S(2)}, u32[]{:S(2)}) collective-permute-start(f32[192,128]{1,0:T(8,128)S(1)} %get-tuple-element.64), channel_id=1, source_target_pairs={{0,2},{2,0},{4,6},{6,4},{8,10},{10,8},{12,14},{14,12},{16,18},{18,... | collective-permute-start | bytes 294920 | tf_op jit(solution)/shard_map/ppermute | solution.py:566
  14.9 1.5 %halo_back.1 = (f32[128,128]{1,0:T(8,128)S(1)}, f32[128,128]{1,0:T(8,128)S(1)}, f32[8,128]{1,0:T(8,128)S(1)}) custom-call(bf16[2,1024,1152]{2,1,0:T(8,128)(2,1)S(1)} %get-tuple-element.65.halo_ref, bf16[2,128,1152]{2,1,0:T(8,128)(2,1)S(1)} %get-tuple-element.70.grad_messages_ref, f32[136,128]{1,0:T(8,128)S(1)} %collective-permute-done.from_pair_ref, ...), custom_call_target="tpu_custom_call" | custom-call | flops 603979776 | bytes 5586944 | tf_op jit(solution)/shard_map/halo_back/pallas_call | solution.py:443
  16.4 0.0 collective-permute-done.2.received_ref
  16.5 1.6 %collective-permute-start.3 = (f32[96,128]{1,0:T(8,128)S(1)}, f32[96,128]{1,0:T(8,128)S(1)}, u32[]{:S(2)}, u32[]{:S(2)}) collective-permute-start(f32[96,128]{1,0:T(8,128)S(1)} %get-tuple-element.76), channel_id=1, source_target_pairs={{0,1},{1,0},{2,3},{3,2},{4,5},{5,4},{6,7},{7,6},{8,9},{9,8},{10,11... | collective-permute-start | bytes 147464 | tf_op jit(solution)/shard_map/ppermute | solution.py:584
  18.0 2.8 %own_back.1 = (f32[128,256]{1,0:T(8,128)S(1)}, f32[16,128]{1,0:T(8,128)S(1)}) custom-call(bf16[4,1024,1152]{2,1,0:T(8,128)(2,1)S(1)} %get-tuple-element.55.local_ref, bf16[2,128,1152]{2,1,0:T(8,128)(2,1)S(1)} %get-tuple-element.70.grad_messages_ref, f32[136,128]{1,0:T(8,128)S(1)} %get-tuple-element.53.pair_ref, f32[136,128]{1,0:T(8,128)S(1)} %get-tuple-element.54.cross_ref, ...), custom_call_target="tpu_custom_call" | custom-call | flops 1207959552 | bytes 10448896 | tf_op jit(solution)/shard_map/own_back/pallas_call | solution.py:443
  20.8 0.0 collective-permute-done.3.received_ref
  20.8 0.7 %collective-permute-start.5 = (f32[128,128]{1,0:T(8,128)S(1)}, f32[128,128]{1,0:T(8,128)S(1)}, u32[]{:S(2)}, u32[]{:S(2)}) collective-permute-start(f32[128,128]{1,0:T(8,128)S(1)} %get-tuple-element.80), channel_id=1, source_target_pairs={{2,4},{4,2},{6,8},{8,6},{10,12},{12,10},{14,16},{16,14},{18,20},{2... | collective-permute-start | bytes 196616 | tf_op jit(solution)/shard_map/ppermute | solution.py:600
  21.5 2.8 %collective-permute-start.4 = (f32[112,128]{1,0:T(8,128)S(1)}, f32[112,128]{1,0:T(8,128)S(1)}, u32[]{:S(2)}, u32[]{:S(2)}) collective-permute-start(f32[112,128]{1,0:T(8,128)S(1)} %join.1), channel_id=1, source_target_pairs={{0,4},{1,5},{2,10},{3,11},{4,0},{5,1},{6,14},{7,15},{8,12},{9,13},... | collective-permute-start | bytes 172040 | tf_op jit(solution)/shard_map/ppermute | solution.py:606
  24.3 2.8 %collective-permute-done.4 = f32[112,128]{1,0:T(8,128)S(1)} collective-permute-done((f32[112,128]{1,0:T(8,128)S(1)}, f32[112,128]{1,0:T(8,128)S(1)}, u32[]{:S(2)}, u32[]{:S(2)}) %collective-permute-start.4) | collective-permute-done | bytes 57376 | tf_op jit(solution)/shard_map/ppermute | solution.py:606
  27.1 0.0 collective-permute-done.5.from_cross_ref
  27.1 0.7 %collective-permute-start.7 = (f32[128,128]{1,0:T(8,128)S(1)}, f32[128,128]{1,0:T(8,128)S(1)}, u32[]{:S(2)}, u32[]{:S(2)}) collective-permute-start(f32[128,128]{1,0:T(8,128)S(1)} %get-tuple-element.83), channel_id=1, source_target_pairs={{0,2},{2,0},{4,6},{6,4},{8,10},{10,8},{12,14},{14,12},{16,18},{18,... | collective-permute-start | bytes 196616 | tf_op jit(solution)/shard_map/ppermute | solution.py:603
  27.8 1.9 %collective-permute-start.6 = (f32[112,128]{1,0:T(8,128)S(1)}, f32[112,128]{1,0:T(8,128)S(1)}, u32[]{:S(2)}, u32[]{:S(2)}) collective-permute-start(f32[112,128]{1,0:T(8,128)S(1)} %add.9), channel_id=1, source_target_pairs={{0,8},{1,9},{2,18},{3,19},{4,12},{5,13},{6,22},{7,23},{8,0},{9,1},... | collective-permute-start | bytes 172040 | tf_op jit(solution)/shard_map/ppermute | solution.py:606
  29.7 2.3 %collective-permute-done.6 = f32[112,128]{1,0:T(8,128)S(1)} collective-permute-done((f32[112,128]{1,0:T(8,128)S(1)}, f32[112,128]{1,0:T(8,128)S(1)}, u32[]{:S(2)}, u32[]{:S(2)}) %collective-permute-start.6) | collective-permute-done | bytes 57376 | tf_op jit(solution)/shard_map/ppermute | solution.py:606
  32.0 0.0 collective-permute-done.7.from_pair_ref
  32.0 3.0 %collective-permute-start.8 = (f32[112,128]{1,0:T(8,128)S(1)}, f32[112,128]{1,0:T(8,128)S(1)}, u32[]{:S(2)}, u32[]{:S(2)}) collective-permute-start(f32[112,128]{1,0:T(8,128)S(1)} %add.10), channel_id=1, source_target_pairs={{0,16},{1,17},{2,6},{3,7},{4,20},{5,21},{6,2},{7,3},{8,24},{9,25},... | collective-permute-start | bytes 172040 | tf_op jit(solution)/shard_map/ppermute | solution.py:606
  35.0 2.2 %collective-permute-done.8 = f32[112,128]{1,0:T(8,128)S(1)} collective-permute-done((f32[112,128]{1,0:T(8,128)S(1)}, f32[112,128]{1,0:T(8,128)S(1)}, u32[]{:S(2)}, u32[]{:S(2)}) %collective-permute-start.8) | collective-permute-done | bytes 57376 | tf_op jit(solution)/shard_map/ppermute | solution.py:606
  37.2 1.2 %collective-permute-start.9 = (f32[112,128]{1,0:T(8,128)S(1)}, f32[112,128]{1,0:T(8,128)S(1)}, u32[]{:S(2)}, u32[]{:S(2)}) collective-permute-start(f32[112,128]{1,0:T(8,128)S(1)} %add.11.mine_ref), channel_id=1, source_target_pairs={{0,1},{1,0},{2,3},{3,2},{4,5},{5,4},{6,7},{7,6},{8,9},{9,8},{10,11... | collective-permute-start | bytes 172040 | tf_op jit(solution)/shard_map/ppermute | solution.py:610
  38.4 3.0 %collective-permute-done.9.other_ref = f32[112,128]{1,0:T(8,128)S(1)} collective-permute-done((f32[112,128]{1,0:T(8,128)S(1)}, f32[112,128]{1,0:T(8,128)S(1)}, u32[]{:S(2)}, u32[]{:S(2)}) %collective-permute-start.9) | collective-permute-done | bytes 57376 | tf_op jit(solution)/shard_map/ppermute | solution.py:610
  41.4 0.1 collective-permute-start.10
  41.5 0.7 %fold.1 = (f32[1,128,256]{2,1,0:T(8,128)}, f32[1,256]{1,0:T(1,128)}) custom-call(f32[128,256]{1,0:T(8,128)S(1)} %get-tuple-element.74.own_ref, f32[128,128]{1,0:T(8,128)S(1)} %collective-permute-done.7.from_pair_ref, f32[128,128]{1,0:T(8,128)S(1)} %collective-permute-done.5.from_cross_ref, f32[1,256]{1,0:T(1,128)S(1)} %get-tuple-element.86.energy_in_ref), custom_call_target="tpu_custom_call" | custom-call | bytes 395264 | tf_op jit(solution)/shard_map/fold/pallas_call | solution.py:443
  42.2 0.6 %collective-permute-done.10.other_ref = f32[208,128]{1,0:T(8,128)S(1)} collective-permute-done((f32[208,128]{1,0:T(8,128)S(1)}, f32[208,128]{1,0:T(8,128)S(1)}, u32[]{:S(2)}, u32[]{:S(2)}) %collective-permute-start.10) | collective-permute-done | bytes 106528 | tf_op jit(solution)/shard_map/ppermute | solution.py:622
  42.8 0.7 %finish.1 = (f32[8,128]{1,0:T(8,128)}, f32[384,128]{1,0:T(8,128)}, f32[1,128]{1,0:T(1,128)}, f32[1,8]{1,0:T(1,128)}) custom-call(f32[208,128]{1,0:T(8,128)S(1)} %gather.1.mine_ref, f32[208,128]{1,0:T(8,128)S(1)} %collective-permute-done.10.other_ref), custom_call_target="tpu_custom_call" | custom-call | bytes 414240 | tf_op jit(solution)/shard_map/finish/pallas_call | solution.py:443
  (6 shorter events, 0.1 us)
Async XLA Ops:
  1.8 6.2 %collective-permute-start = (f32[136,128]{1,0:T(8,128)S(1)}, f32[136,128]{1,0:T(8,128)S(1)}, u32[]{:S(2)}, u32[]{:S(2)}) collective-permute-start(f32[136,128]{1,0:T(8,128)S(1)} %get-tuple-element.53.pair_ref), channel_id=1, source_target_pairs={{0,2},{2,0},{4,6},{6,4},{8,10},{10,8},{12,14},{14,12},{16,18},{18,... | collective-permute-start | bytes 208904 | tf_op jit(solution)/shard_map/ppermute | solution.py:512
  2.3 5.7 %collective-permute-start.1 = (f32[136,128]{1,0:T(8,128)S(1)}, f32[136,128]{1,0:T(8,128)S(1)}, u32[]{:S(2)}, u32[]{:S(2)}) collective-permute-start(f32[136,128]{1,0:T(8,128)S(1)} %get-tuple-element.54.cross_ref), channel_id=1, source_target_pairs={{2,4},{4,2},{6,8},{8,6},{10,12},{12,10},{14,16},{16,14},{18,20},{2... | collective-permute-start | bytes 208904 | tf_op jit(solution)/shard_map/ppermute | solution.py:511
  11.0 5.4 %collective-permute-start.2 = (f32[192,128]{1,0:T(8,128)S(1)}, f32[192,128]{1,0:T(8,128)S(1)}, u32[]{:S(2)}, u32[]{:S(2)}) collective-permute-start(f32[192,128]{1,0:T(8,128)S(1)} %get-tuple-element.64), channel_id=1, source_target_pairs={{0,2},{2,0},{4,6},{6,4},{8,10},{10,8},{12,14},{14,12},{16,18},{18,... | collective-permute-start | bytes 294920 | tf_op jit(solution)/shard_map/ppermute | solution.py:566
  16.5 4.3 %collective-permute-start.3 = (f32[96,128]{1,0:T(8,128)S(1)}, f32[96,128]{1,0:T(8,128)S(1)}, u32[]{:S(2)}, u32[]{:S(2)}) collective-permute-start(f32[96,128]{1,0:T(8,128)S(1)} %get-tuple-element.76), channel_id=1, source_target_pairs={{0,1},{1,0},{2,3},{3,2},{4,5},{5,4},{6,7},{7,6},{8,9},{9,8},{10,11... | collective-permute-start | bytes 147464 | tf_op jit(solution)/shard_map/ppermute | solution.py:584
  20.8 6.3 %collective-permute-start.5 = (f32[128,128]{1,0:T(8,128)S(1)}, f32[128,128]{1,0:T(8,128)S(1)}, u32[]{:S(2)}, u32[]{:S(2)}) collective-permute-start(f32[128,128]{1,0:T(8,128)S(1)} %get-tuple-element.80), channel_id=1, source_target_pairs={{2,4},{4,2},{6,8},{8,6},{10,12},{12,10},{14,16},{16,14},{18,20},{2... | collective-permute-start | bytes 196616 | tf_op jit(solution)/shard_map/ppermute | solution.py:600
  21.5 5.6 %collective-permute-start.4 = (f32[112,128]{1,0:T(8,128)S(1)}, f32[112,128]{1,0:T(8,128)S(1)}, u32[]{:S(2)}, u32[]{:S(2)}) collective-permute-start(f32[112,128]{1,0:T(8,128)S(1)} %join.1), channel_id=1, source_target_pairs={{0,4},{1,5},{2,10},{3,11},{4,0},{5,1},{6,14},{7,15},{8,12},{9,13},... | collective-permute-start | bytes 172040 | tf_op jit(solution)/shard_map/ppermute | solution.py:606
  27.1 4.9 %collective-permute-start.7 = (f32[128,128]{1,0:T(8,128)S(1)}, f32[128,128]{1,0:T(8,128)S(1)}, u32[]{:S(2)}, u32[]{:S(2)}) collective-permute-start(f32[128,128]{1,0:T(8,128)S(1)} %get-tuple-element.83), channel_id=1, source_target_pairs={{0,2},{2,0},{4,6},{6,4},{8,10},{10,8},{12,14},{14,12},{16,18},{18,... | collective-permute-start | bytes 196616 | tf_op jit(solution)/shard_map/ppermute | solution.py:603
  27.8 4.2 %collective-permute-start.6 = (f32[112,128]{1,0:T(8,128)S(1)}, f32[112,128]{1,0:T(8,128)S(1)}, u32[]{:S(2)}, u32[]{:S(2)}) collective-permute-start(f32[112,128]{1,0:T(8,128)S(1)} %add.9), channel_id=1, source_target_pairs={{0,8},{1,9},{2,18},{3,19},{4,12},{5,13},{6,22},{7,23},{8,0},{9,1},... | collective-permute-start | bytes 172040 | tf_op jit(solution)/shard_map/ppermute | solution.py:606
  32.0 5.1 %collective-permute-start.8 = (f32[112,128]{1,0:T(8,128)S(1)}, f32[112,128]{1,0:T(8,128)S(1)}, u32[]{:S(2)}, u32[]{:S(2)}) collective-permute-start(f32[112,128]{1,0:T(8,128)S(1)} %add.10), channel_id=1, source_target_pairs={{0,16},{1,17},{2,6},{3,7},{4,20},{5,21},{6,2},{7,3},{8,24},{9,25},... | collective-permute-start | bytes 172040 | tf_op jit(solution)/shard_map/ppermute | solution.py:606
  37.2 4.2 %collective-permute-start.9 = (f32[112,128]{1,0:T(8,128)S(1)}, f32[112,128]{1,0:T(8,128)S(1)}, u32[]{:S(2)}, u32[]{:S(2)}) collective-permute-start(f32[112,128]{1,0:T(8,128)S(1)} %add.11.mine_ref), channel_id=1, source_target_pairs={{0,1},{1,0},{2,3},{3,2},{4,5},{5,4},{6,7},{7,6},{8,9},{9,8},{10,11... | collective-permute-start | bytes 172040 | tf_op jit(solution)/shard_map/ppermute | solution.py:610
  41.4 1.4 %collective-permute-start.10 = (f32[208,128]{1,0:T(8,128)S(1)}, f32[208,128]{1,0:T(8,128)S(1)}, u32[]{:S(2)}, u32[]{:S(2)}) collective-permute-start(f32[208,128]{1,0:T(8,128)S(1)} %gather.1.mine_ref), channel_id=1, source_target_pairs={{0,2},{2,0},{4,6},{6,4},{8,10},{10,8},{12,14},{14,12},{16,18},{18,... | collective-permute-start | bytes 319496 | tf_op jit(solution)/shard_map/ppermute | solution.py:622
where the time goes:
time: 43.7 us; the launch traced here: 43.5 us
  starting transfers between devices  17.1 us (39%)
  Pallas kernels  14.2 us (32%)
  waiting for transfers between devices  10.8 us (25%)
  between operations  1.43 us (3%)
    pallas_call x8, Pallas kernels, call(): pl.pallas_call(kernel, out_shape=shapes, in_specs=[vmem] * len(inputs), o...  8.57 us
    ppermute x3, starting transfers between devices, body(): value = value + lax.ppermute(value, ('space', 'dp'), route)  7.76 us
    ppermute x3, waiting for transfers between devices, body(): value = value + lax.ppermute(value, ('space', 'dp'), route)  7.17 us
    pallas_call x1, Pallas kernels, body(): pl.pallas_call(local_kernel, out_shape=(jax.ShapeDtypeStruct((len(LOCAL),...  4.4 us
    ppermute x1, starting transfers between devices, body(): received = lax.ppermute(sent, 'space', pair)  3.96 us
    ppermute x1, waiting for transfers between devices, body(): lax.ppermute(value, 'dp', across)  3.05 us
    ppermute x1, starting transfers between devices, body(): received = lax.ppermute(sent, 'dp', across)  1.56 us
    ppermute x1, starting transfers between devices, body(): lax.ppermute(value, 'dp', across)  1.2 us
  transfers between devices with their start and end apart: 11, of which 5 were waited for; matrix products, arithmetic and copies ran while one was open for 0% of the time, Pallas kernels for 21%

commit v1 on v0

--- a/solution.py
+++ b/solution.py
@@ -402,9 +402,9 @@
     out_ref[HALF:, :] = mine_ref[QUARTER:, :] + other_ref[QUARTER:, :]
 
 
-def fold_kernel(own_ref, from_pair_ref, from_cross_ref, energy_in_ref, grad_ref, energy_ref):
+def fold_kernel(own_ref, pair_low_ref, pair_high_ref, from_cross_ref, energy_in_ref, grad_ref, energy_ref):
     even = lax.axis_index("space") % 2 == 0
-    pair = from_pair_ref[...]
+    pair = jnp.concatenate([pair_low_ref[...], pair_high_ref[...]], axis=0)
     cross = from_cross_ref[...]
     grad_ref[0, :, :GROUP] = own_ref[:, :GROUP] + jnp.where(even, cross, pair)
     grad_ref[0, :, GROUP:] = own_ref[:, GROUP:] + jnp.where(even, pair, cross)
@@ -425,15 +425,22 @@
 def exchange_routes(space, dp):
     steps = [(1 << k, 0) for k in range(1, space.bit_length() - 1)]
     steps += [(0, 1 << k) for k in range(1, dp.bit_length() - 1)]
-    routes = []
-    for turn in range(len(steps)):
-        route = []
-        for s in range(space):
-            across, along = steps[(turn + s % 2) % len(steps)]
-            for d in range(dp):
-                route.append((s * dp + d, (s ^ across) * dp + (d ^ along)))
-        routes.append(route)
-    return routes
+    rounds = []
+    for turn in range(0, len(steps), 2):
+        kinds = ((0,), (1,), (0, 1)) if turn + 1 < len(steps) else ((0,),)
+        routes = []
+        for kind in kinds:
+            route = []
+            for s in range(space):
+                across = along = 0
+                for k in kind:
+                    step = steps[(turn + k + 1 - s % 2) % len(steps)]
+                    across, along = across ^ step[0], along ^ step[1]
+                for d in range(dp):
+                    route.append((s * dp + d, (s ^ across) * dp + (d ^ along)))
+            routes.append(route)
+        rounds.append(routes)
+    return rounds
 
 
 def call(kernel, name, inputs, outputs, mib=4, scratch=(), flops=0):
@@ -594,26 +601,32 @@
     (value,) = call(
         join_kernel, "join", (quarter, received, joined), (((QUARTER + REST, CH), f32),)
     )
-    for turn, route in enumerate(exchange_routes(space, dp)):
-        if turn == 0:
+    everyone = ("space", "dp")
+    rounds = exchange_routes(space, dp)
+    for turn, routes in enumerate(rounds):
+        if turn == len(rounds) - 1:
+            value = jnp.pad(value, ((0, CH + 8 - value.shape[0]), (0, 0)))
             value, cross_grad = lax.optimization_barrier((value, cross_grad))
             cross_grad = lax.ppermute(cross_grad, "space", cross)
-        if turn == 1:
-            value, cross_grad, pair_grad = lax.optimization_barrier((value, cross_grad, pair_grad))
-            pair_grad = lax.ppermute(pair_grad, "space", pair)
-        if turn == 2:
-            value, pair_grad = lax.optimization_barrier((value, pair_grad))
-        value = value + lax.ppermute(value, ("space", "dp"), route)
+        arrived = [lax.ppermute(value, everyone, route) for route in routes]
+        value = value + arrived[0]
+        if len(arrived) == 3:
+            value = value + (arrived[1] + arrived[2])
+    value = value[: QUARTER + REST]
+    value, cross_grad, pair_grad = lax.optimization_barrier((value, cross_grad, pair_grad))
+    halves = [lax.ppermute(pair_grad[k : k + CH // 2], "space", pair) for k in (0, CH // 2)]
+    other = lax.ppermute(value, "dp", across)
+    other, pair_low, pair_high = lax.optimization_barrier((other, *halves))
     (value,) = call(
         gather_kernel,
         "gather",
-        (value, lax.ppermute(value, "dp", across)),
+        (value, other),
         (((HALF + REST, CH), f32),),
     )
     feature_grad, energy = call(
         fold_kernel,
         "fold",
-        (own_grad, pair_grad, cross_grad, energy),
+        (own_grad, pair_low, pair_high, cross_grad, energy),
         (((1, CH, atoms_here), f32), ((1, atoms_here), f32)),
     )
     radial_grad, mix_grad, readout_grad, shift_grad = call(

time: 43.7 us -> 42.3 us (0.968)
  the two profiles are of different devices: /device:TPU:0 before, /device:TPU:7 now
where the time goes in v1:
time: 42.3 us; the launch traced here: 42.1 us
  starting transfers between devices  21.2 us (50%)
  Pallas kernels  14.2 us (34%)
  waiting for transfers between devices  5.28 us (12%)
  between operations  1.43 us (3%)
    pallas_call x8, Pallas kernels, call(): pl.pallas_call(kernel, out_shape=shapes, in_specs=[vmem] * len(inputs), o...  8.58 us
    ppermute x4, starting transfers between devices, body(): arrived = [lax.ppermute(value, everyone, route) for route in routes]  5.8 us
    ppermute x1, starting transfers between devices, body(): cross_grad = lax.ppermute(cross_grad, 'space', cross)  5.44 us
    pallas_call x1, Pallas kernels, body(): pl.pallas_call(local_kernel, out_shape=(jax.ShapeDtypeStruct((len(LOCAL),...  4.4 us
    ppermute x1, starting transfers between devices, body(): from_cross = lax.ppermute(to_cross, 'space', cross)  3.05 us
    ppermute x1, starting transfers between devices, body(): lax.ppermute(value, 'space', pair)  2.95 us
    ppermute x2, starting transfers between devices, body(): lax.ppermute(pair_grad[k:k + CH // 2], 'space', pair)  2.36 us
    ppermute x4, waiting for transfers between devices, body(): arrived = [lax.ppermute(value, everyone, route) for route in routes]  1.95 us
  transfers between devices with their start and end apart: 13, of which 6 were waited for; matrix products, arithmetic and copies ran while one was open for 0% of the time, Pallas kernels for 22%

profile of v1, /device:TPU:7, one launch (start us, length us, event | category | flops | bytes accessed | tf_op | source)
XLA Modules:
  0.0 42.1 jit_solution(4117926984032334131)
XLA Ops:
  0.6 1.2 %split.1 = (f32[136,128]{1,0:T(8,128)S(1)}, f32[136,128]{1,0:T(8,128)S(1)}, s32[1,20]{1,0:T(1,128)S(1)}, s32[1,20]{1,0:T(1,128)S(1)}, s32[1,256]{1,0:T(1,128)S(1...) custom-call(f32[1,128,256]{2,1,0:T(8,128)} %refs_0_.1, ...), custom_call_target="tpu_custom_call" | custom-call | tf_op jit(solution)/shard_map/split/pallas_call | solution.py:501
  1.8 0.7 %collective-permute-start = (f32[136,128]{1,0:T(8,128)S(1)}, f32[136,128]{1,0:T(8,128)S(1)}, u32[]{:S(2)}, u32[]{:S(2)}) collective-permute-start(f32[136,128]{1,0:T(8,128)S(1)} %get-tuple-element.54.pair_ref), channel_id=1, source_target_pairs={{0,2},{2,0},{4,6},{6,4},{8,10},{10,8},{12,14},{14,12},{16,18},{18,... | collective-permute-start | bytes 208904 | tf_op jit(solution)/shard_map/ppermute | solution.py:519
  2.6 3.0 %collective-permute-start.1 = (f32[136,128]{1,0:T(8,128)S(1)}, f32[136,128]{1,0:T(8,128)S(1)}, u32[]{:S(2)}, u32[]{:S(2)}) collective-permute-start(f32[136,128]{1,0:T(8,128)S(1)} %get-tuple-element.55.cross_ref), channel_id=1, source_target_pairs={{2,4},{4,2},{6,8},{8,6},{10,12},{12,10},{14,16},{16,14},{18,20},{2... | collective-permute-start | bytes 208904 | tf_op jit(solution)/shard_map/ppermute | solution.py:518
  6.3 4.4 %local_pairs.1 = (bf16[4,1024,1152]{2,1,0:T(8,128)(2,1)S(1)}, f32[2,128,1152]{2,1,0:T(8,128)S(1)}, f32[8,128]{1,0:T(8,128)S(1)}) custom-call(s32[1,1]{1,0:T(1,128)S(6)} %copy.17.count_ref, s32[1,20]{1,0:T(1,128)S(1)} %get-tuple-element.51.pair_target_ref, s32[1,20]{1,0:T(1,128)S(1)} %get-tuple-element.52.pair_source_ref, ...), custom_call_target="tpu_custom_call" | custom-call | flops 1207959552 | bytes 14000000 | tf_op jit(solution)/shard_map/local_pairs/pallas_call | solution.py:522
  10.7 0.0 collective-permute-done.from_pair_ref
  10.7 0.0 collective-permute-done.1.from_cross_ref
  10.7 2.9 %node_stage.1 = (f32[1,256]{1,0:T(1,128)S(1)}, f32[128,256]{1,0:T(8,128)S(1)}, f32[192,128]{1,0:T(8,128)S(1)}, f32[192,128]{1,0:T(8,128)S(1)}, f32[8,128]{1,0:T(...) custom-call(f32[136,128]{1,0:T(8,128)S(1)} %get-tuple-element.54.pair_ref, ...), custom_call_target="tpu_custom_call" | custom-call | flops 603979776 | bytes 7208480 | tf_op jit(solution)/shard_map/node_stage/pallas_call | solution.py:450
  13.6 0.1 collective-permute-start.2
  13.7 1.5 %halo_back.1 = (f32[128,128]{1,0:T(8,128)S(1)}, f32[128,128]{1,0:T(8,128)S(1)}, f32[8,128]{1,0:T(8,128)S(1)}) custom-call(bf16[2,1024,1152]{2,1,0:T(8,128)(2,1)S(1)} %get-tuple-element.66.halo_ref, bf16[2,128,1152]{2,1,0:T(8,128)(2,1)S(1)} %get-tuple-element.71.grad_messages_ref, f32[136,128]{1,0:T(8,128)S(1)} %collective-permute-done.from_pair_ref, ...), custom_call_target="tpu_custom_call" | custom-call | flops 603979776 | bytes 5586944 | tf_op jit(solution)/shard_map/halo_back/pallas_call | solution.py:450
  15.2 0.0 collective-permute-done.2.received_ref
  15.2 0.3 collective-permute-start.3
  15.5 2.8 %own_back.1 = (f32[128,256]{1,0:T(8,128)S(1)}, f32[16,128]{1,0:T(8,128)S(1)}) custom-call(bf16[4,1024,1152]{2,1,0:T(8,128)(2,1)S(1)} %get-tuple-element.56.local_ref, bf16[2,128,1152]{2,1,0:T(8,128)(2,1)S(1)} %get-tuple-element.71.grad_messages_ref, f32[136,128]{1,0:T(8,128)S(1)} %get-tuple-element.54.pair_ref, f32[136,128]{1,0:T(8,128)S(1)} %get-tuple-element.55.cross_ref, ...), custom_call_target="tpu_custom_call" | custom-call | flops 1207959552 | bytes 10448896 | tf_op jit(solution)/shard_map/own_back/pallas_call | solution.py:450
  18.3 0.0 collective-permute-done.3.received_ref
  18.3 1.6 %collective-permute-start.6 = (f32[112,128]{1,0:T(8,128)S(1)}, f32[112,128]{1,0:T(8,128)S(1)}, u32[]{:S(2)}, u32[]{:S(2)}) collective-permute-start(f32[112,128]{1,0:T(8,128)S(1)} %join.1), channel_id=1, source_target_pairs={{0,24},{1,25},{2,14},{3,15},{4,28},{5,29},{6,10},{7,11},{8,16},{9,... | collective-permute-start | bytes 172040 | tf_op jit(solution)/shard_map/ppermute | solution.py:611
  20.0 0.0 collective-permute-start.5
  20.0 1.1 %collective-permute-start.4 = (f32[112,128]{1,0:T(8,128)S(1)}, f32[112,128]{1,0:T(8,128)S(1)}, u32[]{:S(2)}, u32[]{:S(2)}) collective-permute-start(f32[112,128]{1,0:T(8,128)S(1)} %join.1), channel_id=1, source_target_pairs={{0,8},{1,9},{2,6},{3,7},{4,12},{5,13},{6,2},{7,3},{8,0},{9,1},{10,... | collective-permute-start | bytes 172040 | tf_op jit(solution)/shard_map/ppermute | solution.py:611
  21.0 1.3 %collective-permute-done.6 = f32[112,128]{1,0:T(8,128)S(1)} collective-permute-done((f32[112,128]{1,0:T(8,128)S(1)}, f32[112,128]{1,0:T(8,128)S(1)}, u32[]{:S(2)}, u32[]{:S(2)}) %collective-permute-start.6) | collective-permute-done | bytes 57376 | tf_op jit(solution)/shard_map/ppermute | solution.py:611
  22.3 0.7 %collective-permute-done.5 = f32[112,128]{1,0:T(8,128)S(1)} collective-permute-done((f32[112,128]{1,0:T(8,128)S(1)}, f32[112,128]{1,0:T(8,128)S(1)}, u32[]{:S(2)}, u32[]{:S(2)}) %collective-permute-start.5) | collective-permute-done | bytes 57376 | tf_op jit(solution)/shard_map/ppermute | solution.py:611
  23.0 0.0 collective-permute-done.4
  23.0 3.1 %collective-permute-start.7 = (f32[136,128]{1,0:T(8,128)S(1)}, f32[136,128]{1,0:T(8,128)S(1)}, u32[]{:S(2)}, u32[]{:S(2)}) collective-permute-start(f32[136,128]{1,0:T(8,128)S(1)} %pad.4), channel_id=1, source_target_pairs={{0,4},{1,5},{2,18},{3,19},{4,0},{5,1},{6,22},{7,23},{8,12},{9,13},... | collective-permute-start | bytes 208904 | tf_op jit(solution)/shard_map/ppermute | solution.py:611
  26.1 5.4 %collective-permute-start.8 = (f32[128,128]{1,0:T(8,128)S(1)}, f32[128,128]{1,0:T(8,128)S(1)}, u32[]{:S(2)}, u32[]{:S(2)}) collective-permute-start(f32[128,128]{1,0:T(8,128)S(1)} %get-tuple-element.81), channel_id=1, source_target_pairs={{2,4},{4,2},{6,8},{8,6},{10,12},{12,10},{14,16},{16,14},{18,20},{2... | collective-permute-start | bytes 196616 | tf_op jit(solution)/shard_map/ppermute | solution.py:610
  31.6 0.0 collective-permute-done.7
  31.6 1.9 %collective-permute-done.8.from_cross_ref = f32[128,128]{1,0:T(8,128)S(1)} collective-permute-done((f32[128,128]{1,0:T(8,128)S(1)}, f32[128,128]{1,0:T(8,128)S(1)}, u32[]{:S(2)}, u32[]{:S(2)}) %collective-permute-start.8) | collective-permute-done | bytes 65568 | tf_op jit(solution)/shard_map/ppermute | solution.py:610
  33.5 0.4 %collective-permute-start.9 = (f32[112,128]{1,0:T(8,128)S(1)}, f32[112,128]{1,0:T(8,128)S(1)}, u32[]{:S(2)}, u32[]{:S(2)}) collective-permute-start(f32[112,128]{1,0:T(8,128)S(1)} %slice_add_fusion.mine_ref), channel_id=1, source_target_pairs={{0,1},{1,0},{2,3},{3,2},{4,5},{5,4},{6,7},{7,6},{8,9},{9,8},{10,11... | collective-permute-start | bytes 172040 | tf_op jit(solution)/shard_map/ppermute | solution.py:618
  34.0 2.3 %collective-permute-start.11 = (f32[64,128]{1,0:T(8,128)S(1)}, f32[64,128]{1,0:T(8,128)S(1)}, u32[]{:S(2)}, u32[]{:S(2)}) collective-permute-start(f32[64,128]{1,0:T(8,128)S(1)} %get-tuple-element.96), channel_id=1, source_target_pairs={{0,2},{2,0},{4,6},{6,4},{8,10},{10,8},{12,14},{14,12},{16,18},{18,... | collective-permute-start | bytes 98312 | tf_op jit(solution)/shard_map/ppermute | solution.py:617
  36.2 0.1 collective-permute-start.10
  36.3 0.8 %collective-permute-done.11.pair_high_ref = f32[64,128]{1,0:T(8,128)S(1)} collective-permute-done((f32[64,128]{1,0:T(8,128)S(1)}, f32[64,128]{1,0:T(8,128)S(1)}, u32[]{:S(2)}, u32[]{:S(2)}) %collective-permute-start.11) | collective-permute-done | bytes 32800 | tf_op jit(solution)/shard_map/ppermute | solution.py:617
  37.1 0.3 collective-permute-done.10.pair_low_ref
  37.4 0.0 collective-permute-done.9.other_ref
  37.5 2.9 %collective-permute-start.12 = (f32[208,128]{1,0:T(8,128)S(1)}, f32[208,128]{1,0:T(8,128)S(1)}, u32[]{:S(2)}, u32[]{:S(2)}) collective-permute-start(f32[208,128]{1,0:T(8,128)S(1)} %gather.1.mine_ref), channel_id=1, source_target_pairs={{0,2},{2,0},{4,6},{6,4},{8,10},{10,8},{12,14},{14,12},{16,18},{18,... | collective-permute-start | bytes 319496 | tf_op jit(solution)/shard_map/ppermute | solution.py:635
  40.4 0.7 %fold.1 = (f32[1,128,256]{2,1,0:T(8,128)}, f32[1,256]{1,0:T(1,128)}) custom-call(f32[128,256]{1,0:T(8,128)S(1)} %get-tuple-element.75.own_ref, f32[64,128]{1,0:T(8,128)S(1)} %collective-permute-done.10.pair_low_ref, f32[64,128]{1,0:T(8,128)S(1)} %collective-permute-done.11.pair_high_ref, f32[128,128]{1,0:T(8,128)S(1)} %collective-permute-done.8.from_cross_ref, ...), custom_call_target="tpu_custom_call" | custom-call | bytes 395264 | tf_op jit(solution)/shard_map/fold/pallas_call | solution.py:450
  41.1 0.3 collective-permute-done.12.other_ref
  41.4 0.7 %finish.1 = (f32[8,128]{1,0:T(8,128)}, f32[384,128]{1,0:T(8,128)}, f32[1,128]{1,0:T(1,128)}, f32[1,8]{1,0:T(1,128)}) custom-call(f32[208,128]{1,0:T(8,128)S(1)} %gather.1.mine_ref, f32[208,128]{1,0:T(8,128)S(1)} %collective-permute-done.12.other_ref), custom_call_target="tpu_custom_call" | custom-call | bytes 414240 | tf_op jit(solution)/shard_map/finish/pallas_call | solution.py:450
  (7 shorter events, 0.1 us)
Async XLA Ops:
  1.8 8.8 %collective-permute-start = (f32[136,128]{1,0:T(8,128)S(1)}, f32[136,128]{1,0:T(8,128)S(1)}, u32[]{:S(2)}, u32[]{:S(2)}) collective-permute-start(f32[136,128]{1,0:T(8,128)S(1)} %get-tuple-element.54.pair_ref), channel_id=1, source_target_pairs={{0,2},{2,0},{4,6},{6,4},{8,10},{10,8},{12,14},{14,12},{16,18},{18,... | collective-permute-start | bytes 208904 | tf_op jit(solution)/shard_map/ppermute | solution.py:519
  2.6 8.1 %collective-permute-start.1 = (f32[136,128]{1,0:T(8,128)S(1)}, f32[136,128]{1,0:T(8,128)S(1)}, u32[]{:S(2)}, u32[]{:S(2)}) collective-permute-start(f32[136,128]{1,0:T(8,128)S(1)} %get-tuple-element.55.cross_ref), channel_id=1, source_target_pairs={{2,4},{4,2},{6,8},{8,6},{10,12},{12,10},{14,16},{16,14},{18,20},{2... | collective-permute-start | bytes 208904 | tf_op jit(solution)/shard_map/ppermute | solution.py:518
  13.6 1.6 %collective-permute-start.2 = (f32[192,128]{1,0:T(8,128)S(1)}, f32[192,128]{1,0:T(8,128)S(1)}, u32[]{:S(2)}, u32[]{:S(2)}) collective-permute-start(f32[192,128]{1,0:T(8,128)S(1)} %get-tuple-element.65), channel_id=1, source_target_pairs={{0,2},{2,0},{4,6},{6,4},{8,10},{10,8},{12,14},{14,12},{16,18},{18,... | collective-permute-start | bytes 294920 | tf_op jit(solution)/shard_map/ppermute | solution.py:573
  15.2 3.1 %collective-permute-start.3 = (f32[96,128]{1,0:T(8,128)S(1)}, f32[96,128]{1,0:T(8,128)S(1)}, u32[]{:S(2)}, u32[]{:S(2)}) collective-permute-start(f32[96,128]{1,0:T(8,128)S(1)} %get-tuple-element.77), channel_id=1, source_target_pairs={{0,1},{1,0},{2,3},{3,2},{4,5},{5,4},{6,7},{7,6},{8,9},{9,8},{10,11... | collective-permute-start | bytes 147464 | tf_op jit(solution)/shard_map/ppermute | solution.py:591
  18.3 4.0 %collective-permute-start.6 = (f32[112,128]{1,0:T(8,128)S(1)}, f32[112,128]{1,0:T(8,128)S(1)}, u32[]{:S(2)}, u32[]{:S(2)}) collective-permute-start(f32[112,128]{1,0:T(8,128)S(1)} %join.1), channel_id=1, source_target_pairs={{0,24},{1,25},{2,14},{3,15},{4,28},{5,29},{6,10},{7,11},{8,16},{9,... | collective-permute-start | bytes 172040 | tf_op jit(solution)/shard_map/ppermute | solution.py:611
  20.0 3.0 %collective-permute-start.5 = (f32[112,128]{1,0:T(8,128)S(1)}, f32[112,128]{1,0:T(8,128)S(1)}, u32[]{:S(2)}, u32[]{:S(2)}) collective-permute-start(f32[112,128]{1,0:T(8,128)S(1)} %join.1), channel_id=1, source_target_pairs={{0,16},{1,17},{2,10},{3,11},{4,20},{5,21},{6,14},{7,15},{8,24},{9,... | collective-permute-start | bytes 172040 | tf_op jit(solution)/shard_map/ppermute | solution.py:611
  20.0 3.0 %collective-permute-start.4 = (f32[112,128]{1,0:T(8,128)S(1)}, f32[112,128]{1,0:T(8,128)S(1)}, u32[]{:S(2)}, u32[]{:S(2)}) collective-permute-start(f32[112,128]{1,0:T(8,128)S(1)} %join.1), channel_id=1, source_target_pairs={{0,8},{1,9},{2,6},{3,7},{4,12},{5,13},{6,2},{7,3},{8,0},{9,1},{10,... | collective-permute-start | bytes 172040 | tf_op jit(solution)/shard_map/ppermute | solution.py:611
  23.0 8.5 %collective-permute-start.7 = (f32[136,128]{1,0:T(8,128)S(1)}, f32[136,128]{1,0:T(8,128)S(1)}, u32[]{:S(2)}, u32[]{:S(2)}) collective-permute-start(f32[136,128]{1,0:T(8,128)S(1)} %pad.4), channel_id=1, source_target_pairs={{0,4},{1,5},{2,18},{3,19},{4,0},{5,1},{6,22},{7,23},{8,12},{9,13},... | collective-permute-start | bytes 208904 | tf_op jit(solution)/shard_map/ppermute | solution.py:611
  26.1 7.4 %collective-permute-start.8 = (f32[128,128]{1,0:T(8,128)S(1)}, f32[128,128]{1,0:T(8,128)S(1)}, u32[]{:S(2)}, u32[]{:S(2)}) collective-permute-start(f32[128,128]{1,0:T(8,128)S(1)} %get-tuple-element.81), channel_id=1, source_target_pairs={{2,4},{4,2},{6,8},{8,6},{10,12},{12,10},{14,16},{16,14},{18,20},{2... | collective-permute-start | bytes 196616 | tf_op jit(solution)/shard_map/ppermute | solution.py:610
  33.5 3.9 %collective-permute-start.9 = (f32[112,128]{1,0:T(8,128)S(1)}, f32[112,128]{1,0:T(8,128)S(1)}, u32[]{:S(2)}, u32[]{:S(2)}) collective-permute-start(f32[112,128]{1,0:T(8,128)S(1)} %slice_add_fusion.mine_ref), channel_id=1, source_target_pairs={{0,1},{1,0},{2,3},{3,2},{4,5},{5,4},{6,7},{7,6},{8,9},{9,8},{10,11... | collective-permute-start | bytes 172040 | tf_op jit(solution)/shard_map/ppermute | solution.py:618
  34.0 3.1 %collective-permute-start.11 = (f32[64,128]{1,0:T(8,128)S(1)}, f32[64,128]{1,0:T(8,128)S(1)}, u32[]{:S(2)}, u32[]{:S(2)}) collective-permute-start(f32[64,128]{1,0:T(8,128)S(1)} %get-tuple-element.96), channel_id=1, source_target_pairs={{0,2},{2,0},{4,6},{6,4},{8,10},{10,8},{12,14},{14,12},{16,18},{18,... | collective-permute-start | bytes 98312 | tf_op jit(solution)/shard_map/ppermute | solution.py:617
  36.2 1.2 %collective-permute-start.10 = (f32[64,128]{1,0:T(8,128)S(1)}, f32[64,128]{1,0:T(8,128)S(1)}, u32[]{:S(2)}, u32[]{:S(2)}) collective-permute-start(f32[64,128]{1,0:T(8,128)S(1)} %get-tuple-element.97), channel_id=1, source_target_pairs={{0,2},{2,0},{4,6},{6,4},{8,10},{10,8},{12,14},{14,12},{16,18},{18,... | collective-permute-start | bytes 98312 | tf_op jit(solution)/shard_map/ppermute | solution.py:617
  37.5 3.9 %collective-permute-start.12 = (f32[208,128]{1,0:T(8,128)S(1)}, f32[208,128]{1,0:T(8,128)S(1)}, u32[]{:S(2)}, u32[]{:S(2)}) collective-permute-start(f32[208,128]{1,0:T(8,128)S(1)} %gather.1.mine_ref), channel_id=1, source_target_pairs={{0,2},{2,0},{4,6},{6,4},{8,10},{10,8},{12,14},{14,12},{16,18},{18,... | collective-permute-start | bytes 319496 | tf_op jit(solution)/shard_map/ppermute | solution.py:635
